TPU v7x, 32 devices: a whole 2x2x4 slice. The times are simulated.
32 devices in a mesh: tiles: 2 (over y), acq: 8 (over z, x), pix: 2 (over core).
Axes of the slice: x: 2, y: 2, z: 4, core: 2. Of those that a mesh axis runs over, the one named last changes fastest.
Arguments:
- slc: bfloat16 [32, 2, 32, 256], P('acq', None, ('tiles', 'pix')), parts along dimension 2, may hold values from -6 to 6
- disp: bfloat16 [32, 32, 256], P('acq', ('tiles', 'pix')), parts along dimension 1, may hold values from -3 to 3
- times: bfloat16 [32], P('acq'), may hold values from 0 to 4
- velocity: float32 [32, 256], P(('tiles', 'pix')), parts along dimension 0, may hold values from -4 to 4
- amplitude: float32 [32, 256], P(('tiles', 'pix')), parts along dimension 0, may hold values from 0.1 to 1
- pair_ends: int32 [512, 2], P('acq'), may hold values from 0 to 31, as said below
Outputs:
- slc_grad: float32 [32, 2, 32, 256], P('acq', None, ('tiles', 'pix')), parts along dimension 2
- disp_grad: float32 [32, 32, 256], P('acq', ('tiles', 'pix')), parts along dimension 1
There are 2 independent parts, one for each index of `tiles`. A program takes and returns all parts, laid end to end along the dimension named above; an argument that names none is the same for every part. Nothing has to cross between parts.
Inputs may be any that keep to these rules, and one draw needn't show every extreme that they name: `pair_ends`: each row names two different acquisitions. Among the 128 endpoints of one aligned block of 64 rows, at most 16 lie in any run of 4 acquisitions that starts at a multiple of 4, and some run holds exactly 16 in every block.
All inputs are finite; a program needn't handle non-finite values.
Results may differ from a plain program's by a relative error of at most 0.0003.
Values may be sent and summed in bfloat16 or wider, within the bound.
A program may use at most 64 MiB of HBM per device.

v0:
```python
import jax
import jax.numpy as jnp
from jax import lax
from jax.sharding import PartitionSpec as P

LOOK = 2


def with_halo(shard, sides, width):
    for axis, dim in sides:
        size, length = (lax.axis_size(axis), shard.shape[dim])
        up = [(i, (i + 1) % size) for i in range(size - 1)]
        down = [(j, i) for i, j in up]
        last = lax.slice_in_dim(shard, length - width, length, axis=dim)
        first = lax.slice_in_dim(shard, 0, width, axis=dim)
        before = lax.ppermute(last, axis, up)
        after = lax.ppermute(first, axis, down)
        shard = jnp.concatenate([before, shard, after], axis=dim)
    return shard


def window_mean(extended, look):
    row_count = extended.shape[-2] - 2 * look
    col_count = extended.shape[-1]
    window = 2 * look + 1
    padded = jnp.pad(extended, [(0, 0)] * (extended.ndim - 1) + [(look, look)])
    summed = jnp.zeros(extended.shape[:-2] + (row_count, col_count), jnp.float32)
    for offset_row in range(window):
        for offset_col in range(window):
            summed = (
                summed
                + padded[
                    ..., offset_row : offset_row + row_count, offset_col : offset_col + col_count
                ]
            )
    return summed / float(window * window)


def residual_of(ref_ext, sec_ext, phase, amplitude, look):
    ref_re, ref_im = (ref_ext[:, 0], ref_ext[:, 1])
    sec_re, sec_im = (sec_ext[:, 0], sec_ext[:, 1])
    inter = jnp.stack([ref_re * sec_re + ref_im * sec_im, ref_im * sec_re - ref_re * sec_im], 1)
    looked = window_mean(inter, look)
    model_re = jnp.cos(phase)
    model_im = jnp.sin(phase)
    resid = looked - amplitude[None, None] * jnp.stack([model_re, model_im], 1)
    misfit_q = amplitude[None] * (resid[:, 0] * model_im - resid[:, 1] * model_re)
    return (resid, misfit_q)


def endpoint_terms(adjoint, ref_own, sec_own, misfit_q):
    grad_re, grad_im = (adjoint[:, 0], adjoint[:, 1])
    ref_re, ref_im = (ref_own[:, 0], ref_own[:, 1])
    sec_re, sec_im = (sec_own[:, 0], sec_own[:, 1])
    ref_term = jnp.stack(
        [grad_re * sec_re - grad_im * sec_im, grad_re * sec_im + grad_im * sec_re, -misfit_q], 1
    )
    sec_term = jnp.stack(
        [grad_re * ref_re + grad_im * ref_im, grad_re * ref_im - grad_im * ref_re, misfit_q], 1
    )
    return (ref_term, sec_term)


def per_device(slc, disp, times, velocity, amplitude, pair_ends):
    look = LOOK
    acq_local = slc.shape[0]
    row_count = slc.shape[2]
    col_count = slc.shape[3]
    pair_count = pair_ends.shape[0]
    ext_rows = row_count + 2 * look
    packed = jnp.concatenate([slc, disp[:, None]], axis=1)
    extended = with_halo(packed, (("pix", 2),), look)
    flat = extended.reshape(acq_local, 3 * ext_rows * col_count)
    endpoints = jnp.concatenate([pair_ends[:, 0], pair_ends[:, 1]])
    piece_data = lax.all_gather(flat, "acq", axis=0, tiled=True)
    piece_time = lax.all_gather(times, "acq", axis=0, tiled=True)
    count = piece_data.shape[0]
    pick = (endpoints[:, None] == jnp.arange(count, dtype=jnp.int32)[None, :]).astype(jnp.bfloat16)
    end_data = jnp.dot(pick, piece_data, preferred_element_type=jnp.float32)
    end_time = jnp.dot(pick, piece_time, preferred_element_type=jnp.float32)
    end_data = end_data.reshape(2 * pair_count, 3, ext_rows, col_count)
    ref_ext = end_data[:pair_count, :2]
    sec_ext = end_data[pair_count:, :2]
    ref_disp = end_data[:pair_count, 2, look : look + row_count]
    sec_disp = end_data[pair_count:, 2, look : look + row_count]
    phase = (
        (end_time[pair_count:] - end_time[:pair_count])[:, None, None] * velocity[None]
        + sec_disp
        - ref_disp
    )
    resid, misfit_q = residual_of(ref_ext, sec_ext, phase, amplitude, look)
    resid_ext = with_halo(resid, (("pix", 2),), look)
    adjoint = window_mean(resid_ext, look)
    ref_term, sec_term = endpoint_terms(
        adjoint,
        ref_ext[:, :, look : look + row_count],
        sec_ext[:, :, look : look + row_count],
        misfit_q,
    )
    contrib = jnp.concatenate([ref_term, sec_term], axis=0).reshape(
        2 * pair_count, 3 * row_count * col_count
    )
    pick = (
        endpoints[None, :] == jnp.arange(acq_local * lax.axis_size("acq"), dtype=jnp.int32)[:, None]
    ).astype(jnp.float32)
    summed = lax.psum_scatter(
        jnp.dot(pick, contrib, precision=lax.Precision.HIGHEST, preferred_element_type=jnp.float32),
        "acq",
        scatter_dimension=0,
        tiled=True,
    )
    summed = summed.reshape(acq_local, 3, row_count, col_count)
    return (summed[:, :2], summed[:, 2])


def solution(mesh):
    return jax.shard_map(
        per_device,
        mesh=mesh,
        in_specs=(
            P("acq", None, ("tiles", "pix"), None),
            P("acq", ("tiles", "pix"), None),
            P("acq"),
            P(("tiles", "pix"), None),
            P(("tiles", "pix"), None),
            P("acq", None),
        ),
        out_specs=(P("acq", None, ("tiles", "pix"), None), P("acq", ("tiles", "pix"), None)),
        check_vma=False,
    )
```

profile of v0, /device:TPU:0, one launch (start us, length us, event | category | flops | bytes accessed | tf_op | source)
XLA Modules:
  0.0 191.0 jit_solution(4587850754133298521)
XLA Ops:
  7.2 0.0 all-reduce.6.cloned.1.call-start
  7.2 0.9 pad_maximum_fusion.5
  8.1 2.4 %collective-permute-start = (bf16[4,3,2,256]{3,2,1,0:T(2,128)(2,1)S(1)}, bf16[4,3,2,256]{3,2,1,0:T(2,128)(2,1)S(1)}, u32[]{:S(2)}, u32[]{:S(2)}) collective-permute-start(bf16[4,3,2,256]{3,2,1,0:T(2,128)(2,1)S(1)} %get-tuple-element.14), channel_id=1, source_target_pairs={{0,1},{2,3},{4,5},{6,7},{8,9},{10,11},{12,13},{14,15},{16,17},{18,... | collective-permute-start | bytes 36872 | tf_op jit(solution)/shard_map/ppermute | solution.py:16
  10.4 1.3 fusion.69
  12.4 0.9 dynamic-update-slice
  13.3 1.3 collective-permute-start.1
  14.6 22.5 %all-reduce.2 = bf16[32]{0:T(256)(128)(2,1)S(1)} all-reduce(bf16[32]{0:T(256)(128)(2,1)S(1)} %dynamic-update-slice), channel_id=1, replica_groups=mesh['tiles'=2,'acq'=8,'pix'=2] {'acq'}, use_global_device_ids=true, to_apply=%add.2 | all-reduce | flops 32 | bytes 128
  37.1 0.8 slice_bitcast_fusion.2
  37.8 0.1 pad_add_fusion
  37.9 0.2 convolution_bitcast_fusion
  38.1 0.1 slice_subtract_fusion.1
  38.2 0.0 collective-permute-done
  38.2 0.0 collective-permute-done.1
  38.2 0.8 pad_maximum_fusion.3
  39.1 31.6 %all-gather = bf16[8,4,9216]{2,1,0:T(4,128)(2,1)S(1)} all-gather(bf16[1,4,9216]{2,1,0:T(4,128)(2,1)S(1)} %reshape.32), channel_id=1, replica_groups=mesh['tiles'=2,'acq'=8,'pix'=2] {'acq'}, dimensions={0}, use_global_device_ids=true | all-gather | bytes 663552 | tf_op jit(solution)/shard_map/all_gather | solution.py:75
  70.7 0.1 reshape.33
  70.8 1.1 fusion.60
  71.9 0.0 copy-start
  71.9 0.0 copy-start.7
  71.9 0.9 multiply_add_fusion
  72.8 1.2 copy-done
  74.0 0.0 copy-done.7
  74.0 4.1 %fusion.58 = (f32[64,1,8,256]{0,3,2,1:T(8,128)S(1)}, f32[64,1,8,256]{0,3,2,1:T(8,128)S(1)}) fusion(f32[128,3,12,256]{0,3,2,1:T(8,128)S(1)} %bitcast.28, f32[8,256]{1,0:T(8,128)S(1)} %copy-done.7, f32[64]{0:T(128)S(1)} %slice_subtract_fusion.1), kind=kLoop, calls=%fused_computation.100 | loop fusion | flops 393216 | bytes 2105600 | tf_op jit(solution)/shard_map/sin | solution.py:45
  78.1 0.0 copy-start.6
  78.1 0.3 pad_maximum_fusion
  78.5 0.4 copy-done.6
  78.8 6.0 %fusion.54 = f32[64,2,8,256]{0,3,2,1:T(8,128)S(1)} fusion(f32[64,1,8,256]{0,3,2,1:T(8,128)S(1)} %get-tuple-element.8, f32[64,1,8,256]{0,3,2,1:T(8,128)S(1)} %get-tuple-element.9, f32[64,2,12,256]{0,3,2,1:T(8,128)S(1)} %pad_maximum_fusion, f32[64,1,12,256]{0,3,2,1:T(8,128)S(1)} %get-tuple-element.11, f32[64,1,12,256]{0,3,2,1:T(8,128)S(1)} %get-tuple-element.10, ...), kind=kLoop, calls=%fused_computation.78 | loop fusion | flops 8650752 | bytes 5251072 | tf_op jit(solution)/shard_map/sub | solution.py:46
  84.9 0.0 copy-start.1
  84.9 0.1 fusion.68
  85.0 1.3 collective-permute-start.2
  86.3 1.5 collective-permute-start.3
  87.8 1.7 fusion.66
  89.5 0.0 collective-permute-done.2
  89.5 0.0 copy-start.4
  89.5 0.6 collective-permute-done.3
  90.1 0.0 copy-done.1
  90.1 0.2 copy-done.4
  90.3 0.0 copy-start.5
  90.3 0.8 copy-done.5
  91.1 0.4 select_maximum_fusion
  91.4 10.1 %fusion.10 = f32[64,2,8,256]{0,3,2,1:T(8,128)} fusion(f32[64,2,8,256]{0,3,2,1:T(8,128)} %copy-done.1, f32[64,2,2,256]{0,3,2,1:T(8,128)} %copy-done.5, f32[64,2,2,256]{0,3,2,1:T(8,128)} %copy-done.4, f32[64,2,12,260]{0,3,2,1:T(8,128)S(1)} %select_maximum_fusion), kind=kLoop, calls=%fused_computation.30 | loop fusion | flops 7602176 | bytes 23592960 | tf_op jit(solution)/shard_map/div | solution.py:36
  101.6 0.0 copy-start.2
  101.6 0.0 copy-start.3
  101.6 3.7 %multiply_subtract_fusion.2 = (f32[64,1,8,256]{0,3,2,1:T(8,128)S(1)}, f32[64,1,8,256]{0,3,2,1:T(8,128)S(1)}, f32[64,1,8,256]{0,3,2,1:T(8,128)S(1)}, f32[64,1,8,256]{0,3,2,1:T(8,128)S(1)}) fusion(f32[128,3,12,256]{0,3,2,1:T(8,128)} %bitcast.29, f32[64,2,8,256]{0,3,2,1:T(8,128)} %fusion.10), kind=kLoop, calls=%fused_computation.99 | loop fusion | flops 1572864 | bytes 5242880 | tf_op jit(solution)/shard_map/sub | solution.py:56
  105.3 0.0 copy-done.2
  105.3 0.0 copy-done.3
  105.3 0.9 maximum_maximum_fusion
  106.2 2.7 %fusion.63 = f32[32,6144]{1,0:T(8,128)} fusion(f32[128,6144]{0,1:T(8,128)S(1)} %bitcast.30, s32[128]{0:T(128)S(1)} %pad_add_fusion), kind=kOutput, calls=%fused_computation.110 | convolution fusion | flops 301993984 | bytes 3932672 | tf_op jit(solution)/shard_map/dot_general | solution.py:107
  109.0 0.0 all-reduce.6.cloned.1.call-update
  109.6 72.3 %all-reduce.6.cloned.1.call-done = f32[32,6144]{1,0:T(8,128)} async-done(((f32[32,6144]{1,0:T(8,128)}), f32[32,6144]{1,0:T(8,128)}) %all-reduce.6.cloned.1.call-update) | async-done | bytes 786448
  181.9 0.9 constant_dynamic-slice_fusion
  182.9 0.6 slice_bitcast_fusion
  183.5 0.6 slice.371
  (3 shorter events, 0.1 us)
Async XLA Ops:
  7.2 174.8 %all-reduce.6.cloned.1.call-start = ((), (), s32[]{:S(2)}) async-start(), calls=%async_computation | async-start | bytes 1572864
  8.1 30.1 %collective-permute-start = (bf16[4,3,2,256]{3,2,1,0:T(2,128)(2,1)S(1)}, bf16[4,3,2,256]{3,2,1,0:T(2,128)(2,1)S(1)}, u32[]{:S(2)}, u32[]{:S(2)}) collective-permute-start(bf16[4,3,2,256]{3,2,1,0:T(2,128)(2,1)S(1)} %get-tuple-element.14), channel_id=1, source_target_pairs={{0,1},{2,3},{4,5},{6,7},{8,9},{10,11},{12,13},{14,15},{16,17},{18,... | collective-permute-start | bytes 36872 | tf_op jit(solution)/shard_map/ppermute | solution.py:16
  13.3 24.9 %collective-permute-start.1 = (bf16[4,3,2,256]{3,2,1,0:T(2,128)(2,1)S(1)}, bf16[4,3,2,256]{3,2,1,0:T(2,128)(2,1)S(1)}, u32[]{:S(2)}, u32[]{:S(2)}) collective-permute-start(bf16[4,3,2,256]{3,2,1,0:T(2,128)(2,1)S(1)} %get-tuple-element.15), channel_id=1, source_target_pairs={{1,0},{3,2},{5,4},{7,6},{9,8},{11,10},{13,12},{15,14},{17,16},{19,... | collective-permute-start | bytes 36872 | tf_op jit(solution)/shard_map/ppermute | solution.py:17
  71.9 2.1 %copy-start = (f32[128,9216]{0,1:T(8,128)}, f32[128,9216]{0,1:T(8,128)S(1)}, u32[]{:S(2)}) copy-start(f32[128,9216]{0,1:T(8,128)S(1)} %fusion.60) | copy-start | bytes 14155780
  71.9 2.1 %copy-start.7 = (f32[8,256]{1,0:T(8,128)S(1)}, f32[8,256]{1,0:T(8,128)}, u32[]{:S(2)}) copy-start(f32[8,256]{1,0:T(8,128)} %param.9) | copy-start | bytes 24580
  78.1 0.7 copy-start.6
  84.9 5.2 %copy-start.1 = (f32[64,2,8,256]{0,3,2,1:T(8,128)}, f32[64,2,8,256]{0,3,2,1:T(8,128)S(1)}, u32[]{:S(2)}) copy-start(f32[64,2,8,256]{0,3,2,1:T(8,128)S(1)} %fusion.54) | copy-start | bytes 3145732
  85.0 4.5 %collective-permute-start.2 = (f32[64,2,2,256]{0,3,2,1:T(8,128)S(1)}, f32[64,2,2,256]{0,3,2,1:T(8,128)S(1)}, u32[]{:S(2)}, u32[]{:S(2)}) collective-permute-start(f32[64,2,2,256]{0,3,2,1:T(8,128)S(1)} %get-tuple-element.12), channel_id=1, source_target_pairs={{0,1},{2,3},{4,5},{6,7},{8,9},{10,11},{12,13},{14,15},{16,17},{18,... | collective-permute-start | bytes 786440 | tf_op jit(solution)/shard_map/ppermute | solution.py:16
  86.3 3.8 %collective-permute-start.3 = (f32[64,2,2,256]{0,3,2,1:T(8,128)S(1)}, f32[64,2,2,256]{0,3,2,1:T(8,128)S(1)}, u32[]{:S(2)}, u32[]{:S(2)}) collective-permute-start(f32[64,2,2,256]{0,3,2,1:T(8,128)S(1)} %get-tuple-element.13), channel_id=1, source_target_pairs={{1,0},{3,2},{5,4},{7,6},{9,8},{11,10},{13,12},{15,14},{17,16},{19,... | collective-permute-start | bytes 786440 | tf_op jit(solution)/shard_map/ppermute | solution.py:17
  89.5 0.8 copy-start.4
  90.3 0.8 copy-start.5
  101.6 3.8 %copy-start.2 = (f32[64,1,8,256]{0,3,2,1:T(8,128)S(1)}, f32[64,1,8,256]{0,3,2,1:T(8,128)}, u32[]{:S(2)}) copy-start(f32[64,1,8,256]{0,3,2,1:T(8,128)} %get-tuple-element.2) | copy-start | bytes 1572868
  101.6 3.8 %copy-start.3 = (f32[64,1,8,256]{0,3,2,1:T(8,128)S(1)}, f32[64,1,8,256]{0,3,2,1:T(8,128)}, u32[]{:S(2)}) copy-start(f32[64,1,8,256]{0,3,2,1:T(8,128)} %get-tuple-element.3) | copy-start | bytes 1572868
Sparse Core Ops, SparseCore 0:
  109.1 72.7 all-reduce.5
where the time goes:
time: 192 us; the launch traced here: 191 us
  waiting for transfers between devices  73 us (38%)
  blocking collectives  54.1 us (28%)
  other arithmetic  30 us (16%)
  between operations  15.5 us (8%)
  local copies, waits for them, and re-layouts  7.98 us (4%)
  starting transfers between devices  6.47 us (3%)
  matrix products  4.02 us (2%)
    unnamed x2, waiting for transfers between devices  72.3 us
    all_gather x1, blocking collectives, per_device(): piece_data = lax.all_gather(flat, 'acq', axis=0, tiled=True)  31.6 us
    unnamed x1, blocking collectives  22.5 us
    div x1, other arithmetic, window_mean(): return summed / float(window * window)  10.1 us
    sub x1, other arithmetic, residual_of(): resid = looked - amplitude[None, None] * jnp.stack([model_re, model_im], 1)  6.04 us
    unnamed x23, local copies, waits for them, and re-layouts  5.9 us
    sin x1, other arithmetic, residual_of(): model_im = jnp.sin(phase)  4.11 us
  transfers between devices with their start and end apart: 5, of which 2 were waited for; matrix products, arithmetic and copies ran while one was open for 3% of the time, Pallas kernels for 0%

commit v1 on v0

v1 whole, which is shorter than its diff:
```python
import functools
import math

import jax
import jax.numpy as jnp
from jax import lax
from jax.experimental import pallas as pl
from jax.experimental.pallas import tpu as pltpu
from jax.sharding import PartitionSpec as P

LOOK = 2
GROUP = 2
HALO = 2 * LOOK
LANES = 128
MESH = pl.DeviceIdType.MESH
F32 = jnp.float32
BF16 = jnp.bfloat16
TAU_HI = 6.28125
TAU_LO = 2.0 * math.pi - TAU_HI


def cos_sin(angle):
    turns = jnp.floor(angle * (0.5 / math.pi) + 0.5)
    half = 0.5 * ((angle - turns * TAU_HI) - turns * TAU_LO)
    sq = half * half
    sin_half = jnp.full_like(sq, -1.0 / math.factorial(11))
    for order, sign in ((9, 1.0), (7, -1.0), (5, 1.0), (3, -1.0), (1, 1.0)):
        sin_half = sin_half * sq + sign / math.factorial(order)
    sin_half = sin_half * half
    cos_half = jnp.full_like(sq, 1.0 / math.factorial(12))
    for order, sign in ((10, -1.0), (8, 1.0), (6, -1.0), (4, 1.0), (2, -1.0), (0, 1.0)):
        cos_half = cos_half * sq + sign / math.factorial(order)
    return 1.0 - 2.0 * sin_half * sin_half, 2.0 * sin_half * cos_half


def row_box(values, count):
    pairs = [values[i] + values[i + 1] for i in range(len(values) - 1)]
    out = []
    for i in range(count):
        low = max(0, i - LOOK)
        total, at = None, low
        while at <= i + LOOK:
            if at < i + LOOK:
                piece, at = pairs[at], at + 2
            else:
                piece, at = values[at], at + 1
            total = piece if total is None else total + piece
        out.append(total)
    return out


def put_split(ref, base, values, cols):
    for i in range(0, len(values), 2):
        both = jnp.concatenate([values[i], values[i + 1]], axis=0)
        high = both.astype(BF16)
        low = (both - high.astype(F32)).astype(BF16)
        at = pl.ds(pl.multiple_of(base + 8 * i, 16), 16)
        ref[at, 0:cols] = high
        ref[at, cols : 2 * cols] = low


def kernel(
    n, al, rows, cols, lanes,
    slc_ref, disp_ref, times_ref, vel_ref, amp_ref, ends_ref,
    grad_ref, dgrad_ref,
    rx, oth, msg, msgr, vah, stg, stg_o, zre, zim, ure, uim, velb, ampb,
    zab, aub, band, lhs, filt, acc, qacc, weights,
    msg_send, msg_recv, va_send, va_recv,
    own_send, blk_recv, xf_send, of_send, oth_recv,
):
    me = lax.axis_index("acq")
    pix = lax.axis_index("pix")
    zcount = n // GROUP
    mz = me // GROUP
    mx = me % GROUP
    blk_rows = 3 * al * rows
    slc_rows = 2 * al * rows
    wide = 3 * rows
    ext = rows + HALO
    mid = rows + LOOK
    halves = cols // LANES
    nbr = mz * GROUP + (GROUP - 1 - mx)
    core = {"pix": 1 - pix}

    def peer(step):
        return (me + step) % n

    barrier = pltpu.get_barrier_semaphore()
    for step in range(1, n):
        pl.semaphore_signal(barrier, inc=1, device_id={"acq": peer(step)}, device_id_type=MESH)
    pl.semaphore_signal(barrier, inc=1, device_id=core, device_id_type=MESH)

    rx[me, 0:slc_rows, :] = slc_ref[...]
    rx[me, slc_rows:blk_rows, :] = disp_ref[...]
    count = ends_ref.shape[0]
    first = ends_ref[:, 0:1]
    second = ends_ref[:, 1:2]
    lane = lax.broadcasted_iota(jnp.int32, (count, lanes), 1)
    slot = lax.broadcasted_iota(jnp.int32, (count, 8 * n), 1)

    def spread(ids):
        return (ids // al) * 8 + ids % al

    def hot(where):
        return where.astype(F32).astype(BF16)

    contract = (((0,), (0,)), ((), ()))
    counts = lax.dot_general(
        hot(slot == spread(first)), hot(lane == second), contract, preferred_element_type=F32
    ) + lax.dot_general(
        hot(slot == spread(second)), hot(lane == first), contract, preferred_element_type=F32
    )
    t_lane = lax.broadcasted_iota(jnp.int32, (al, lanes), 1)
    t_sub = lax.broadcasted_iota(jnp.int32, (al, lanes), 0)
    t_row = jnp.sum(jnp.where(t_lane == me * al + t_sub, times_ref[...], 0.0), axis=0, keepdims=True)
    m_sub = lax.broadcasted_iota(jnp.int32, (8, lanes), 0)
    t_tile = jnp.where(m_sub == al, jnp.broadcast_to(t_row, (8, lanes)), 0.0)
    for j in range(n):
        msg[j] = counts[8 * j : 8 * j + 8, :] + t_tile
    msgr[me] = msg[me]

    pl.semaphore_wait(barrier, n)

    def block_copy(src, dst, send_sem, recv_sem, device):
        return pltpu.make_async_remote_copy(
            src_ref=src, dst_ref=dst, send_sem=send_sem, recv_sem=recv_sem,
            device_id=device, device_id_type=MESH,
        )

    def own_copy(step):
        to = ((mz + step) % zcount) * GROUP + mx
        if step == 0:
            to = nbr
        return block_copy(rx.at[me], rx.at[me], own_send.at[step], blk_recv.at[me], {"acq": to})

    def core_copy(j):
        return block_copy(rx.at[j], oth.at[j], of_send.at[j], oth_recv.at[j], core)

    def nbr_copy(j):
        return block_copy(rx.at[j], rx.at[j], xf_send.at[j // GROUP], blk_recv.at[j], {"acq": nbr})

    def msg_copy(step):
        to = peer(step)
        return block_copy(msg.at[to], msgr.at[me], msg_send.at[step], msg_recv.at[me], {"acq": to})

    def va_copy(which):
        src = vel_ref if which == 0 else amp_ref
        return block_copy(src, vah.at[which], va_send.at[which], va_recv.at[which], core)

    for step in range(1, zcount):
        own_copy(step).start()
    own_copy(0).start()
    core_copy(me).start()
    for step in range(1, n):
        msg_copy(step).start()
    va_copy(0).start()
    va_copy(1).start()

    at_row = lax.broadcasted_iota(jnp.int32, (2 * cols, cols), 0) % cols
    at_col = lax.broadcasted_iota(jnp.int32, (2 * cols, cols), 1)
    band[...] = hot(jnp.abs(at_row - at_col) <= LOOK)
    acc[...] = jnp.zeros_like(acc)
    qacc[...] = jnp.zeros_like(qacc)

    def own_row(i):
        return i + pix * (rows - 1 - 2 * i)

    def nbr_row(i):
        place = 2 * rows - 1 - i
        return place + (1 - pix) * (rows - 1 - 2 * place)

    va_copy(0).wait_recv()
    va_copy(1).wait_recv()
    for i in range(mid):
        for which, src, dst in ((0, vel_ref, velb), (1, amp_ref, ampb)):
            if i < rows:
                line = src[pl.ds(own_row(i), 1), :]
            else:
                line = vah[which, pl.ds(nbr_row(i), 1), :]
            dst[8 * i : 8 * i + 8, :] = jnp.broadcast_to(line, (8, cols))

    for step in range(1, n):
        msg_copy(step).wait_send()
        frm = peer(step)
        block_copy(msg.at[frm], msgr.at[frm], msg_send.at[step], msg_recv.at[frm], {"acq": frm}).wait_recv()
    weights[...] = functools.reduce(lambda a, b: a + b, [msgr[j] for j in range(n)])

    def zchunk(k):
        return (mz + k) % zcount

    def forward_column(k):
        j = zchunk(k) * GROUP + mx
        nbr_copy(j).wait_recv()
        nbr_copy(j).start()
        core_copy(j).start()

    def forward_nbr(k):
        j = zchunk(k) * GROUP + (GROUP - 1 - mx)
        nbr_copy(j).wait_recv()
        core_copy(j).start()

    def column_of(row, c):
        l8 = lax.broadcasted_iota(jnp.int32, (8, lanes), 1)
        s8 = lax.broadcasted_iota(jnp.int32, (8, lanes), 0)
        line = jnp.broadcast_to(weights[pl.ds(row, 1), :], (8, lanes))
        return jnp.sum(jnp.where(l8 == c * 8 + s8, line, 0.0), axis=1, keepdims=True)

    def unpack(c):
        for src, dst in ((rx, stg), (oth, stg_o)):
            for s in range(GROUP):
                block = src[c * GROUP + s].astype(F32)
                for h in range(halves):
                    part = block[:, h * LANES : (h + 1) * LANES]
                    for a in range(al):
                        base = (s * al + a) * wide
                        dst[h, base : base + 2 * rows, :] = part[a * 2 * rows : (a + 1) * 2 * rows]
                        dst[h, base + 2 * rows : base + wide, :] = part[
                            slc_rows + a * rows : slc_rows + (a + 1) * rows
                        ]

        def take(i, channel):
            src, row = (stg, own_row(i)) if i < rows else (stg_o, nbr_row(i))
            return jnp.concatenate(
                [src[h, pl.ds(channel * rows + row, 8, stride=wide), :] for h in range(halves)], axis=1
            )

        when = column_of(al, c)
        for i in range(ext):
            zre[8 * i : 8 * i + 8, :] = take(i, 0)
            zim[8 * i : 8 * i + 8, :] = take(i, 1)
            if i < mid:
                u_re, u_im = cos_sin(when * velb[8 * i : 8 * i + 8, :] + take(i, 2))
                ure[8 * i : 8 * i + 8, :] = u_re
                uim[8 * i : 8 * i + 8, :] = u_im

    mean = 1.0 / float((2 * LOOK + 1) ** 2)

    def own_ends():
        def one(a, carry):
            for i in range(ext):
                at = pl.ds(8 * i + al * mx + a, 1)
                for ch, src in ((0, zre), (1, zim)):
                    zab[a, ch, 8 * i : 8 * i + 8, :] = jnp.broadcast_to(src[at, :] * mean, (8, cols))
                if i < mid:
                    for ch, src in ((0, ure), (1, uim)):
                        aub[a, ch, 8 * i : 8 * i + 8, :] = (
                            jnp.broadcast_to(src[at, :], (8, cols)) * ampb[8 * i : 8 * i + 8, :]
                        )
            return carry

        lax.fori_loop(0, al, one, 0)

    def tile(i):
        return slice(8 * i, 8 * i + 8)

    def chunk(k, carry):
        c = zchunk(k)
        forward_nbr(k)

        @pl.when(k + 1 < zcount)
        def _():
            forward_column(k + 1)

        for s in range(GROUP):
            core_copy(c * GROUP + s).wait_recv()
        unpack(c)

        @pl.when(k == 0)
        def _():
            own_ends()

        def inter(a, carry):
            re, im = [], []
            for i in range(ext):
                a_re, a_im = zab[a, 0, tile(i), :], zab[a, 1, tile(i), :]
                b_re, b_im = zre[tile(i), :], zim[tile(i), :]
                re.append(a_re * b_re + a_im * b_im)
                im.append(a_im * b_re - a_re * b_im)
            put_split(lhs, a * (2 * 8 * mid), row_box(re, mid), cols)
            put_split(lhs, a * (2 * 8 * mid) + 8 * mid, row_box(im, mid), cols)
            return carry

        lax.fori_loop(0, al, inter, 0)
        filt[...] = jnp.dot(lhs[...], band[...], preferred_element_type=F32)

        def residual(a, carry):
            weight = column_of(a, c)
            base = a * (2 * 8 * mid)
            re, im = [], []
            for i in range(mid):
                a_re, a_im = aub[a, 0, tile(i), :], aub[a, 1, tile(i), :]
                b_re, b_im = ure[tile(i), :], uim[tile(i), :]
                model_re = b_re * a_re + b_im * a_im
                model_im = b_im * a_re - b_re * a_im
                r_re = filt[pl.ds(pl.multiple_of(base + 8 * i, 8), 8), :] - model_re
                r_im = filt[pl.ds(pl.multiple_of(base + 8 * (mid + i), 8), 8), :] - model_im
                if i < rows:
                    qacc[a, tile(i), :] += weight * (r_re * model_im - r_im * model_re)
                re.append(r_re)
                im.append(r_im)
            put_split(lhs, a * (2 * 8 * rows), row_box(re, rows), cols)
            put_split(lhs, a * (2 * 8 * rows) + 8 * rows, row_box(im, rows), cols)
            return carry

        lax.fori_loop(0, al, residual, 0)
        size = al * 2 * 8 * rows
        filt[0:size, :] = jnp.dot(lhs[0:size, :], band[...], preferred_element_type=F32)

        def gradient(a, carry):
            weight = column_of(a, c) * mean
            base = a * (2 * 8 * rows)
            for i in range(rows):
                g_re = filt[pl.ds(pl.multiple_of(base + 8 * i, 8), 8), :]
                g_im = filt[pl.ds(pl.multiple_of(base + 8 * (rows + i), 8), 8), :]
                b_re, b_im = zre[tile(i), :], zim[tile(i), :]
                acc[a, 0, tile(i), :] += weight * (g_re * b_re - g_im * b_im)
                acc[a, 1, tile(i), :] += weight * (g_re * b_im + g_im * b_re)
            return carry

        lax.fori_loop(0, al, gradient, 0)
        return carry

    lax.fori_loop(0, zcount, chunk, 0)

    def finish(a, carry):
        for i in range(rows):
            row = pl.ds(own_row(i), 1)
            for ch in range(2):
                grad_ref[a, ch, row, :] = jnp.sum(acc[a, ch, tile(i), :], axis=0, keepdims=True)
            dgrad_ref[a, row, :] = -jnp.sum(qacc[a, tile(i), :], axis=0, keepdims=True)
        return carry

    lax.fori_loop(0, al, finish, 0)

    for step in range(zcount):
        own_copy(step).wait_send()
    va_copy(0).wait_send()
    va_copy(1).wait_send()

    def drain(j, carry):
        core_copy(j).wait_send()
        return carry

    lax.fori_loop(0, n, drain, 0)

    def drain_nbr(k, carry):
        nbr_copy(zchunk(k) * GROUP + mx).wait_send()
        return carry

    lax.fori_loop(1, zcount, drain_nbr, 0)


def per_device(slc, disp, times, velocity, amplitude, pair_ends):
    al, _, rows, cols = slc.shape
    n = lax.axis_size("acq")
    lanes = -(-(al * n) // LANES) * LANES
    ext, mid = rows + HALO, rows + LOOK
    zcount = n // GROUP
    vmem = pl.BlockSpec(memory_space=pltpu.VMEM)
    dma = pltpu.SemaphoreType.DMA
    scratch = [
        pltpu.VMEM((n, 3 * al * rows, cols), BF16),
        pltpu.VMEM((n, 3 * al * rows, cols), BF16),
        pltpu.VMEM((n, 8, lanes), F32),
        pltpu.VMEM((n, 8, lanes), F32),
        pltpu.VMEM((2, rows, cols), F32),
        pltpu.VMEM((cols // LANES, 8 * 3 * rows, LANES), F32),
        pltpu.VMEM((cols // LANES, 8 * 3 * rows, LANES), F32),
        pltpu.VMEM((8 * ext, cols), F32),
        pltpu.VMEM((8 * ext, cols), F32),
        pltpu.VMEM((8 * mid, cols), F32),
        pltpu.VMEM((8 * mid, cols), F32),
        pltpu.VMEM((8 * mid, cols), F32),
        pltpu.VMEM((8 * mid, cols), F32),
        pltpu.VMEM((al, 2, 8 * ext, cols), F32),
        pltpu.VMEM((al, 2, 8 * mid, cols), F32),
        pltpu.VMEM((2 * cols, cols), BF16),
        pltpu.VMEM((al * 2 * 8 * mid, 2 * cols), BF16),
        pltpu.VMEM((al * 2 * 8 * mid, cols), F32),
        pltpu.VMEM((al, 2, 8 * rows, cols), F32),
        pltpu.VMEM((al, 8 * rows, cols), F32),
        pltpu.VMEM((8, lanes), F32),
        dma((n,)), dma((n,)), dma((2,)), dma((2,)),
        dma((zcount,)), dma((n,)), dma((zcount,)), dma((n,)), dma((n,)),
    ]
    t_wide = jnp.broadcast_to(times.astype(F32)[:, None], (al, lanes))
    return pl.pallas_call(
        functools.partial(kernel, n, al, rows, cols, lanes),
        out_shape=(
            jax.ShapeDtypeStruct((al, 2, rows, cols), F32),
            jax.ShapeDtypeStruct((al, rows, cols), F32),
        ),
        in_specs=[vmem] * 6,
        out_specs=(vmem, vmem),
        scratch_shapes=scratch,
        compiler_params=pltpu.CompilerParams(
            collective_id=0, has_side_effects=True, vmem_limit_bytes=40 * 1024 * 1024
        ),
    )(
        slc.reshape(2 * al * rows, cols),
        disp.reshape(al * rows, cols),
        t_wide, velocity, amplitude, pair_ends,
    )


def solution(mesh):
    return jax.shard_map(
        per_device,
        mesh=mesh,
        in_specs=(
            P("acq", None, ("tiles", "pix"), None),
            P("acq", ("tiles", "pix"), None),
            P("acq"),
            P(("tiles", "pix"), None),
            P(("tiles", "pix"), None),
            P("acq", None),
        ),
        out_specs=(P("acq", None, ("tiles", "pix"), None), P("acq", ("tiles", "pix"), None)),
        check_vma=False,
    )
```

time: 192 us -> 31.1 us (0.16)
  waiting for transfers between devices: 73 us -> 0 us
  blocking collectives: 54.1 us -> 0 us
  other arithmetic: 30 us -> 0 us
  Pallas kernels: 0 us -> 25.1 us
  between operations: 15.5 us -> 0.66 us
  starting transfers between devices: 6.47 us -> 0 us
  matrix products: 4.02 us -> 0 us
  local copies, waits for them, and re-layouts: 7.98 us -> 4.85 us
    unnamed x2 -> x0, waiting for transfers between devices: 72.3 us -> none
    all_gather x1 -> x0, blocking collectives: 31.6 us -> none  [per_device(): piece_data = lax.all_gather(flat, 'acq', axis=0, tiled=True)]
    pallas_call x0 -> x1, Pallas kernels: none -> 25.1 us  [per_device(): pl.pallas_call(functools.partial(kernel, n, al, rows, cols, lanes), out_s...]
    unnamed x1 -> x0, blocking collectives: 22.5 us -> none
    div x1 -> x0, other arithmetic: 10.1 us -> none  [window_mean(): return summed / float(window * window)]
    sub x3 -> x0, other arithmetic: 9.87 us -> none  [the longest x1 6.04 us: residual_of(): resid = looked - amplitude[None, None] * jnp.stack([model_re, model_im], 1)]
    ppermute x4 -> x0, starting transfers between devices: 6.43 us -> none  [the longest x2 3.68 us: with_halo(): before = lax.ppermute(last, axis, up)]
    sin x1 -> x0, other arithmetic: 4.11 us -> none  [residual_of(): model_im = jnp.sin(phase)]
  transfers between devices with their start and end apart: 5 -> 0, of which waited for: 2 -> 0; matrix products, arithmetic and copies ran while one was open for 3% -> 0% of each run, Pallas kernels for 0% -> 0%
where the time goes in v1:
time: 31.1 us; the launch traced here: 30.6 us
  Pallas kernels  25.1 us (81%)
  local copies, waits for them, and re-layouts  4.85 us (16%)
  between operations  0.66 us (2%)
    pallas_call x1, Pallas kernels, per_device(): pl.pallas_call(functools.partial(kernel, n, al, rows, cols, lanes), out_s...  25.1 us
    unnamed x11, local copies, waits for them, and re-layouts  4.12 us
    broadcast_in_dim x1, local copies, waits for them, and re-layouts, per_device(): t_wide = jnp.broadcast_to(times.astype(F32)[:, None], (al, lanes))  0.73 us

profile of v1, /device:TPU:0, one launch (start us, length us, event | category | flops | bytes accessed | tf_op | source)
XLA Modules:
  0.0 30.6 jit_solution(83133181303427623)
XLA Ops:
  0.6 0.0 copy-start
  0.6 0.7 %broadcast_in_dim.2.times_ref = f32[4,128]{1,0:T(4,128)S(1)} broadcast(bf16[4]{0:T(256)(128)(2,1)} %param.8), dimensions={0} | broadcast | bytes 2056 | tf_op jit(solution)/shard_map/broadcast_in_dim | solution.py:386
  1.4 0.8 %copy.8.ends_ref = s32[64,2]{1,0:T(8,128)S(1)} copy(s32[64,2]{0,1:T(2,128)} %param.11) | data formatting | bytes 1024 | tf_op args[5]
  2.1 0.0 copy-done
  2.1 0.0 copy-start.1
  2.1 0.7 %copy-done.1 = bf16[4,8,256]{2,1,0:T(8,128)(2,1)S(1)} copy-done((bf16[4,8,256]{2,1,0:T(8,128)(2,1)S(1)}, bf16[4,8,256]{2,1,0:T(8,128)(2,1)}, u32[]{:S(2)}) %copy-start.1) | copy-done | bytes 16408
  2.9 0.0 copy-start.2
  2.9 0.7 %copy-done.2 = f32[8,256]{1,0:T(8,128)S(1)} copy-done((f32[8,256]{1,0:T(8,128)S(1)}, f32[8,256]{1,0:T(8,128)}, u32[]{:S(2)}) %copy-start.2) | copy-done | bytes 8216
  3.6 0.0 copy-start.3
  3.6 0.7 %copy-done.3 = f32[8,256]{1,0:T(8,128)S(1)} copy-done((f32[8,256]{1,0:T(8,128)S(1)}, f32[8,256]{1,0:T(8,128)}, u32[]{:S(2)}) %copy-start.3) | copy-done | bytes 8216
  4.3 25.1 %shard_map.77 = (f32[4,2,8,256]{3,2,1,0:T(8,128)S(1)}, f32[4,8,256]{2,1,0:T(8,128)S(1)}) custom-call(bf16[64,256]{1,0:T(8,128)(2,1)S(1)} %bitcast.2, bf16[32,256]{1,0:T(8,128)(2,1)S(1)} %bitcast.3, f32[4,128]{1,0:T(4,128)S(1)} %broadcast_in_dim.2.times_ref, f32[8,256]{1,0:T(8,128)S(1)} %copy-done.2, f32[8,256]{1,0:T(8,128)S(1)} %copy-done.3, ...), custom_call_target="tpu_custom_call" | custom-call | tf_op jit(solution)/shard_map/pallas_call | solution.py:387
  29.4 0.6 %copy.11 = f32[4,2,8,256]{3,2,1,0:T(8,128)} copy(f32[4,2,8,256]{3,2,1,0:T(8,128)S(1)} %get-tuple-element.4) | data formatting | bytes 131072
  30.0 0.6 %copy.12 = f32[4,8,256]{2,1,0:T(8,128)} copy(f32[4,8,256]{2,1,0:T(8,128)S(1)} %get-tuple-element.5) | data formatting | bytes 65536
Async XLA Ops:
  0.6 1.5 %copy-start = (bf16[4,2,8,256]{3,2,1,0:T(8,128)(2,1)S(1)}, bf16[4,2,8,256]{3,2,1,0:T(8,128)(2,1)}, u32[]{:S(2)}) copy-start(bf16[4,2,8,256]{3,2,1,0:T(8,128)(2,1)} %param.6) | copy-start | bytes 98308
  2.1 0.7 %copy-start.1 = (bf16[4,8,256]{2,1,0:T(8,128)(2,1)S(1)}, bf16[4,8,256]{2,1,0:T(8,128)(2,1)}, u32[]{:S(2)}) copy-start(bf16[4,8,256]{2,1,0:T(8,128)(2,1)} %param.7) | copy-start | bytes 49156
  2.9 0.7 %copy-start.2 = (f32[8,256]{1,0:T(8,128)S(1)}, f32[8,256]{1,0:T(8,128)}, u32[]{:S(2)}) copy-start(f32[8,256]{1,0:T(8,128)} %vel_ref.1) | copy-start | bytes 24580
  3.6 0.7 %copy-start.3 = (f32[8,256]{1,0:T(8,128)S(1)}, f32[8,256]{1,0:T(8,128)}, u32[]{:S(2)}) copy-start(f32[8,256]{1,0:T(8,128)} %amp_ref.1) | copy-start | bytes 24580

commit v2 on v1

--- a/solution.py
+++ b/solution.py
@@ -61,12 +61,13 @@
 
 def kernel(
     n, al, rows, cols, lanes,
-    slc_ref, disp_ref, times_ref, vel_ref, amp_ref, ends_ref,
+    slc_in, disp_in, times_ref, vel_in, amp_in, ends_in,
     grad_ref, dgrad_ref,
     rx, oth, msg, msgr, vah, stg, stg_o, zre, zim, ure, uim, velb, ampb,
-    zab, aub, band, lhs, filt, acc, qacc, weights,
+    zab, aub, band, lhs, filt, lhs2, filt2, acc, qacc, weights,
     msg_send, msg_recv, va_send, va_recv,
-    own_send, blk_recv, xf_send, of_send, oth_recv,
+    own_send, blk_recv, of_send, oth_recv,
+    vel_ref, amp_ref, ends_ref, in_sem,
 ):
     me = lax.axis_index("acq")
     pix = lax.axis_index("pix")
@@ -79,24 +80,35 @@
     ext = rows + HALO
     mid = rows + LOOK
     halves = cols // LANES
-    nbr = mz * GROUP + (GROUP - 1 - mx)
     core = {"pix": 1 - pix}
 
     def peer(step):
         return (me + step) % n
+
+    loads = [
+        pltpu.make_async_copy(src, dst, in_sem.at[i])
+        for i, (src, dst) in enumerate((
+            (ends_in, ends_ref),
+            (slc_in, rx.at[me, 0:slc_rows, :]),
+            (disp_in, rx.at[me, slc_rows:blk_rows, :]),
+            (vel_in, vel_ref),
+            (amp_in, amp_ref),
+        ))
+    ]
+    for load in loads:
+        load.start()
 
     barrier = pltpu.get_barrier_semaphore()
     for step in range(1, n):
         pl.semaphore_signal(barrier, inc=1, device_id={"acq": peer(step)}, device_id_type=MESH)
     pl.semaphore_signal(barrier, inc=1, device_id=core, device_id_type=MESH)
 
-    rx[me, 0:slc_rows, :] = slc_ref[...]
-    rx[me, slc_rows:blk_rows, :] = disp_ref[...]
-    count = ends_ref.shape[0]
-    first = ends_ref[:, 0:1]
-    second = ends_ref[:, 1:2]
-    lane = lax.broadcasted_iota(jnp.int32, (count, lanes), 1)
-    slot = lax.broadcasted_iota(jnp.int32, (count, 8 * n), 1)
+    loads[0].wait()
+    count = ends_ref.shape[1]
+    first = ends_ref[0:1, :]
+    second = ends_ref[1:2, :]
+    lane = lax.broadcasted_iota(jnp.int32, (lanes, count), 0)
+    slot = lax.broadcasted_iota(jnp.int32, (8 * n, count), 0)
 
     def spread(ids):
         return (ids // al) * 8 + ids % al
@@ -104,7 +116,7 @@
     def hot(where):
         return where.astype(F32).astype(BF16)
 
-    contract = (((0,), (0,)), ((), ()))
+    contract = (((1,), (1,)), ((), ()))
     counts = lax.dot_general(
         hot(slot == spread(first)), hot(lane == second), contract, preferred_element_type=F32
     ) + lax.dot_general(
@@ -119,6 +131,8 @@
         msg[j] = counts[8 * j : 8 * j + 8, :] + t_tile
     msgr[me] = msg[me]
 
+    for load in loads[1:]:
+        load.wait()
     pl.semaphore_wait(barrier, n)
 
     def block_copy(src, dst, send_sem, recv_sem, device):
@@ -128,16 +142,11 @@
         )
 
     def own_copy(step):
-        to = ((mz + step) % zcount) * GROUP + mx
-        if step == 0:
-            to = nbr
+        to = ((mz + step // GROUP) % zcount) * GROUP + (mx + step) % GROUP
         return block_copy(rx.at[me], rx.at[me], own_send.at[step], blk_recv.at[me], {"acq": to})
 
     def core_copy(j):
         return block_copy(rx.at[j], oth.at[j], of_send.at[j], oth_recv.at[j], core)
-
-    def nbr_copy(j):
-        return block_copy(rx.at[j], rx.at[j], xf_send.at[j // GROUP], blk_recv.at[j], {"acq": nbr})
 
     def msg_copy(step):
         to = peer(step)
@@ -147,14 +156,13 @@
         src = vel_ref if which == 0 else amp_ref
         return block_copy(src, vah.at[which], va_send.at[which], va_recv.at[which], core)
 
-    for step in range(1, zcount):
-        own_copy(step).start()
-    own_copy(0).start()
-    core_copy(me).start()
     for step in range(1, n):
         msg_copy(step).start()
+    for step in range(1, n):
+        own_copy(step).start()
     va_copy(0).start()
     va_copy(1).start()
+    core_copy(me).start()
 
     at_row = lax.broadcasted_iota(jnp.int32, (2 * cols, cols), 0) % cols
     at_col = lax.broadcasted_iota(jnp.int32, (2 * cols, cols), 1)
@@ -188,15 +196,9 @@
     def zchunk(k):
         return (mz + k) % zcount
 
-    def forward_column(k):
-        j = zchunk(k) * GROUP + mx
-        nbr_copy(j).wait_recv()
-        nbr_copy(j).start()
-        core_copy(j).start()
-
-    def forward_nbr(k):
-        j = zchunk(k) * GROUP + (GROUP - 1 - mx)
-        nbr_copy(j).wait_recv()
+    def forward(k, s):
+        j = zchunk(k) * GROUP + (mx + s) % GROUP
+        block_copy(rx.at[j], rx.at[j], own_send.at[0], blk_recv.at[j], {"acq": j}).wait_recv()
         core_copy(j).start()
 
     def column_of(row, c):
@@ -250,17 +252,20 @@
 
         lax.fori_loop(0, al, one, 0)
 
+    def columns(src, span):
+        return jnp.dot(src[span, :], band[...], preferred_element_type=F32)
+
     def tile(i):
         return slice(8 * i, 8 * i + 8)
 
     def chunk(k, carry):
         c = zchunk(k)
-        forward_nbr(k)
-
-        @pl.when(k + 1 < zcount)
+
+        @pl.when(k > 0)
         def _():
-            forward_column(k + 1)
-
+            forward(k, 0)
+
+        forward(k, 1)
         for s in range(GROUP):
             core_copy(c * GROUP + s).wait_recv()
         unpack(c)
@@ -269,23 +274,20 @@
         def _():
             own_ends()
 
-        def inter(a, carry):
+        def one(a, carry):
+            weight = jnp.broadcast_to(column_of(a, c), (8, cols))
+            base = a * (2 * 8 * mid)
             re, im = [], []
             for i in range(ext):
                 a_re, a_im = zab[a, 0, tile(i), :], zab[a, 1, tile(i), :]
                 b_re, b_im = zre[tile(i), :], zim[tile(i), :]
                 re.append(a_re * b_re + a_im * b_im)
                 im.append(a_im * b_re - a_re * b_im)
-            put_split(lhs, a * (2 * 8 * mid), row_box(re, mid), cols)
-            put_split(lhs, a * (2 * 8 * mid) + 8 * mid, row_box(im, mid), cols)
-            return carry
-
-        lax.fori_loop(0, al, inter, 0)
-        filt[...] = jnp.dot(lhs[...], band[...], preferred_element_type=F32)
-
-        def residual(a, carry):
-            weight = column_of(a, c)
-            base = a * (2 * 8 * mid)
+            put_split(lhs, base, row_box(re, mid), cols)
+            put_split(lhs, base + 8 * mid, row_box(im, mid), cols)
+            span = pl.ds(pl.multiple_of(base, 16), 2 * 8 * mid)
+            filt[span, :] = columns(lhs, span)
+
             re, im = [], []
             for i in range(mid):
                 a_re, a_im = aub[a, 0, tile(i), :], aub[a, 1, tile(i), :]
@@ -298,26 +300,22 @@
                     qacc[a, tile(i), :] += weight * (r_re * model_im - r_im * model_re)
                 re.append(r_re)
                 im.append(r_im)
-            put_split(lhs, a * (2 * 8 * rows), row_box(re, rows), cols)
-            put_split(lhs, a * (2 * 8 * rows) + 8 * rows, row_box(im, rows), cols)
-            return carry
-
-        lax.fori_loop(0, al, residual, 0)
-        size = al * 2 * 8 * rows
-        filt[0:size, :] = jnp.dot(lhs[0:size, :], band[...], preferred_element_type=F32)
-
-        def gradient(a, carry):
-            weight = column_of(a, c) * mean
             base = a * (2 * 8 * rows)
+            put_split(lhs2, base, row_box(re, rows), cols)
+            put_split(lhs2, base + 8 * rows, row_box(im, rows), cols)
+            span = pl.ds(pl.multiple_of(base, 16), 2 * 8 * rows)
+            filt2[span, :] = columns(lhs2, span)
+
+            weight = weight * mean
             for i in range(rows):
-                g_re = filt[pl.ds(pl.multiple_of(base + 8 * i, 8), 8), :]
-                g_im = filt[pl.ds(pl.multiple_of(base + 8 * (rows + i), 8), 8), :]
+                g_re = filt2[pl.ds(pl.multiple_of(base + 8 * i, 8), 8), :]
+                g_im = filt2[pl.ds(pl.multiple_of(base + 8 * (rows + i), 8), 8), :]
                 b_re, b_im = zre[tile(i), :], zim[tile(i), :]
                 acc[a, 0, tile(i), :] += weight * (g_re * b_re - g_im * b_im)
                 acc[a, 1, tile(i), :] += weight * (g_re * b_im + g_im * b_re)
             return carry
 
-        lax.fori_loop(0, al, gradient, 0)
+        lax.fori_loop(0, al, one, 0, unroll=True)
         return carry
 
     lax.fori_loop(0, zcount, chunk, 0)
@@ -332,7 +330,7 @@
 
     lax.fori_loop(0, al, finish, 0)
 
-    for step in range(zcount):
+    for step in range(1, n):
         own_copy(step).wait_send()
     va_copy(0).wait_send()
     va_copy(1).wait_send()
@@ -342,12 +340,6 @@
         return carry
 
     lax.fori_loop(0, n, drain, 0)
-
-    def drain_nbr(k, carry):
-        nbr_copy(zchunk(k) * GROUP + mx).wait_send()
-        return carry
-
-    lax.fori_loop(1, zcount, drain_nbr, 0)
 
 
 def per_device(slc, disp, times, velocity, amplitude, pair_ends):
@@ -377,12 +369,19 @@
         pltpu.VMEM((2 * cols, cols), BF16),
         pltpu.VMEM((al * 2 * 8 * mid, 2 * cols), BF16),
         pltpu.VMEM((al * 2 * 8 * mid, cols), F32),
+        pltpu.VMEM((al * 2 * 8 * rows, 2 * cols), BF16),
+        pltpu.VMEM((al * 2 * 8 * rows, cols), F32),
         pltpu.VMEM((al, 2, 8 * rows, cols), F32),
         pltpu.VMEM((al, 8 * rows, cols), F32),
         pltpu.VMEM((8, lanes), F32),
         dma((n,)), dma((n,)), dma((2,)), dma((2,)),
-        dma((zcount,)), dma((n,)), dma((zcount,)), dma((n,)), dma((n,)),
+        dma((n,)), dma((n,)), dma((n,)), dma((n,)),
+        pltpu.VMEM((rows, cols), F32),
+        pltpu.VMEM((rows, cols), F32),
+        pltpu.VMEM(pair_ends.shape[::-1], jnp.int32),
+        dma((5,)),
     ]
+    hbm = pl.BlockSpec(memory_space=pltpu.HBM)
     t_wide = jnp.broadcast_to(times.astype(F32)[:, None], (al, lanes))
     return pl.pallas_call(
         functools.partial(kernel, n, al, rows, cols, lanes),
@@ -390,16 +389,16 @@
             jax.ShapeDtypeStruct((al, 2, rows, cols), F32),
             jax.ShapeDtypeStruct((al, rows, cols), F32),
         ),
-        in_specs=[vmem] * 6,
+        in_specs=[hbm, hbm, vmem, hbm, hbm, hbm],
         out_specs=(vmem, vmem),
         scratch_shapes=scratch,
         compiler_params=pltpu.CompilerParams(
-            collective_id=0, has_side_effects=True, vmem_limit_bytes=40 * 1024 * 1024
+            collective_id=0, has_side_effects=True, vmem_limit_bytes=63 * 1024 * 1024
         ),
     )(
         slc.reshape(2 * al * rows, cols),
         disp.reshape(al * rows, cols),
-        t_wide, velocity, amplitude, pair_ends,
+        t_wide, velocity, amplitude, pair_ends.T,
     )
 
 

time: 31.1 us -> 27.7 us (0.89)
  Pallas kernels: 25.1 us -> 23.4 us
  local copies, waits for them, and re-layouts: 4.85 us -> 3.39 us
    pallas_call x1, Pallas kernels: 25.1 us -> 23.4 us  [per_device(): pl.pallas_call(functools.partial(kernel, n, al, rows, cols, lanes), out_s...]
    unnamed x11 -> x6, local copies, waits for them, and re-layouts: 4.12 us -> 2.75 us
where the time goes in v2:
time: 27.7 us; the launch traced here: 27.5 us
  Pallas kernels  23.4 us (84%)
  local copies, waits for them, and re-layouts  3.39 us (12%)
  between operations  0.66 us (2%)
    pallas_call x1, Pallas kernels, per_device(): pl.pallas_call(functools.partial(kernel, n, al, rows, cols, lanes), out_s...  23.4 us
    unnamed x6, local copies, waits for them, and re-layouts  2.75 us
    broadcast_in_dim x1, local copies, waits for them, and re-layouts, per_device(): t_wide = jnp.broadcast_to(times.astype(F32)[:, None], (al, lanes))  0.65 us

profile of v2, /device:TPU:0, one launch (start us, length us, event | category | flops | bytes accessed | tf_op | source)
XLA Modules:
  0.0 27.5 jit_solution(10906736967312546016)
XLA Ops:
  0.6 0.0 copy-start.1
  0.6 0.6 %copy-done.1 = bf16[4]{0:T(256)(128)(2,1)S(1)} copy-done((bf16[4]{0:T(256)(128)(2,1)S(1)}, bf16[4]{0:T(256)(128)(2,1)}, u32[]{:S(2)}) %copy-start.1) | copy-done | bytes 32
  1.3 0.6 %broadcast_in_dim.2.times_ref = f32[4,128]{1,0:T(4,128)} broadcast(bf16[4]{0:T(256)(128)(2,1)S(1)} %copy-done.1), dimensions={0} | broadcast | bytes 2056 | tf_op jit(solution)/shard_map/broadcast_in_dim | solution.py:385
  1.9 23.4 %shard_map.77 = (f32[4,2,8,256]{3,2,1,0:T(8,128)}, f32[4,8,256]{2,1,0:T(8,128)}) custom-call(bf16[64,256]{1,0:T(8,128)(2,1)} %bitcast.3, bf16[32,256]{1,0:T(8,128)(2,1)} %bitcast.4, f32[4,128]{1,0:T(4,128)} %broadcast_in_dim.2.times_ref, f32[8,256]{1,0:T(8,128)} %vel_in.1, f32[8,256]{1,0:T(8,128)} %amp_in.1, s32[2,64]{1,0:T(2,128)} %bitcast.5), custom_call_target="tpu_custom_call" | custom-call | tf_op jit(solution)/shard_map/pallas_call | solution.py:386
  25.4 0.0 copy-start
  25.4 1.5 %copy.10 = f32[4,2,8,256]{3,2,1,0:T(8,128)} copy(f32[4,2,8,256]{3,2,1,0:T(8,128)} %get-tuple-element.4) | data formatting | bytes 131072
  26.8 0.0 copy-done
  26.8 0.6 %copy.11 = f32[4,8,256]{2,1,0:T(8,128)} copy(f32[4,8,256]{2,1,0:T(8,128)S(1)} %copy-done) | data formatting | bytes 65536
Async XLA Ops:
  0.6 0.7 %copy-start.1 = (bf16[4]{0:T(256)(128)(2,1)S(1)}, bf16[4]{0:T(256)(128)(2,1)}, u32[]{:S(2)}) copy-start(bf16[4]{0:T(256)(128)(2,1)} %param.8) | copy-start | bytes 28
  25.4 1.5 %copy-start = (f32[4,8,256]{2,1,0:T(8,128)S(1)}, f32[4,8,256]{2,1,0:T(8,128)}, u32[]{:S(2)}) copy-start(f32[4,8,256]{2,1,0:T(8,128)} %get-tuple-element.5) | copy-start | bytes 98308

commit v3 on v2

--- a/solution.py
+++ b/solution.py
@@ -67,7 +67,7 @@
     zab, aub, band, lhs, filt, lhs2, filt2, acc, qacc, weights,
     msg_send, msg_recv, va_send, va_recv,
     own_send, blk_recv, of_send, oth_recv,
-    vel_ref, amp_ref, ends_ref, in_sem,
+    vel_ref, amp_ref, ends_ref, t_tile, in_sem,
 ):
     me = lax.axis_index("acq")
     pix = lax.axis_index("pix")
@@ -85,6 +85,9 @@
     def peer(step):
         return (me + step) % n
 
+    def zchunk(k):
+        return mz ^ k
+
     loads = [
         pltpu.make_async_copy(src, dst, in_sem.at[i])
         for i, (src, dst) in enumerate((
@@ -122,13 +125,10 @@
     ) + lax.dot_general(
         hot(slot == spread(second)), hot(lane == first), contract, preferred_element_type=F32
     )
-    t_lane = lax.broadcasted_iota(jnp.int32, (al, lanes), 1)
-    t_sub = lax.broadcasted_iota(jnp.int32, (al, lanes), 0)
-    t_row = jnp.sum(jnp.where(t_lane == me * al + t_sub, times_ref[...], 0.0), axis=0, keepdims=True)
-    m_sub = lax.broadcasted_iota(jnp.int32, (8, lanes), 0)
-    t_tile = jnp.where(m_sub == al, jnp.broadcast_to(t_row, (8, lanes)), 0.0)
+    t_tile[...] = jnp.zeros_like(t_tile)
+    t_tile[al : al + 1, 0:al] = times_ref[...].astype(F32)
     for j in range(n):
-        msg[j] = counts[8 * j : 8 * j + 8, :] + t_tile
+        msg[j] = counts[8 * j : 8 * j + 8, :] + t_tile[...]
     msgr[me] = msg[me]
 
     for load in loads[1:]:
@@ -142,7 +142,7 @@
         )
 
     def own_copy(step):
-        to = ((mz + step // GROUP) % zcount) * GROUP + (mx + step) % GROUP
+        to = zchunk(step // GROUP) * GROUP + (mx + step) % GROUP
         return block_copy(rx.at[me], rx.at[me], own_send.at[step], blk_recv.at[me], {"acq": to})
 
     def core_copy(j):
@@ -192,9 +192,6 @@
         frm = peer(step)
         block_copy(msg.at[frm], msgr.at[frm], msg_send.at[step], msg_recv.at[frm], {"acq": frm}).wait_recv()
     weights[...] = functools.reduce(lambda a, b: a + b, [msgr[j] for j in range(n)])
-
-    def zchunk(k):
-        return (mz + k) % zcount
 
     def forward(k, s):
         j = zchunk(k) * GROUP + (mx + s) % GROUP
@@ -226,7 +223,14 @@
                 [src[h, pl.ds(channel * rows + row, 8, stride=wide), :] for h in range(halves)], axis=1
             )
 
-        when = column_of(al, c)
+        t_lane = lax.broadcasted_iota(jnp.int32, (8, lanes), 1)
+        t_sub = lax.broadcasted_iota(jnp.int32, (8, lanes), 0)
+        t_line = jnp.where(
+            t_sub < al,
+            jnp.broadcast_to(msgr[c * GROUP, al : al + 1, :], (8, lanes)),
+            jnp.broadcast_to(msgr[c * GROUP + 1, al : al + 1, :], (8, lanes)),
+        )
+        when = jnp.sum(jnp.where(t_lane == t_sub % al, t_line, 0.0), axis=1, keepdims=True)
         for i in range(ext):
             zre[8 * i : 8 * i + 8, :] = take(i, 0)
             zim[8 * i : 8 * i + 8, :] = take(i, 1)
@@ -379,11 +383,11 @@
         pltpu.VMEM((rows, cols), F32),
         pltpu.VMEM((rows, cols), F32),
         pltpu.VMEM(pair_ends.shape[::-1], jnp.int32),
+        pltpu.VMEM((8, lanes), F32),
         dma((5,)),
     ]
     hbm = pl.BlockSpec(memory_space=pltpu.HBM)
-    t_wide = jnp.broadcast_to(times.astype(F32)[:, None], (al, lanes))
-    return pl.pallas_call(
+    grads = pl.pallas_call(
         functools.partial(kernel, n, al, rows, cols, lanes),
         out_shape=(
             jax.ShapeDtypeStruct((al, 2, rows, cols), F32),
@@ -398,8 +402,9 @@
     )(
         slc.reshape(2 * al * rows, cols),
         disp.reshape(al * rows, cols),
-        t_wide, velocity, amplitude, pair_ends.T,
+        times.reshape(1, al), velocity, amplitude, pair_ends.T,
     )
+    return grads
 
 
 def solution(mesh):

time: 27.7 us -> 24.8 us (0.90)
  Pallas kernels: 23.4 us -> 21.8 us
  local copies, waits for them, and re-layouts: 3.39 us -> 2.1 us
    pallas_call x1, Pallas kernels: 23.4 us -> 21.8 us  [per_device(): pl.pallas_call(functools.partial(kernel, n, al, rows, cols, lanes), out_s...]
    unnamed x6 -> x4, local copies, waits for them, and re-layouts: 2.75 us -> 2.1 us
    broadcast_in_dim x1 -> x0, local copies, waits for them, and re-layouts: 0.65 us -> none  [per_device(): t_wide = jnp.broadcast_to(times.astype(F32)[:, None], (al, lanes))]
where the time goes in v3:
time: 24.8 us; the launch traced here: 24.6 us
  Pallas kernels  21.8 us (88%)
  local copies, waits for them, and re-layouts  2.1 us (8%)
  between operations  0.65 us (3%)
    pallas_call x1, Pallas kernels, per_device(): pl.pallas_call(functools.partial(kernel, n, al, rows, cols, lanes), out_s...  21.8 us
    unnamed x4, local copies, waits for them, and re-layouts  2.1 us

profile of v3, /device:TPU:0, one launch (start us, length us, event | category | flops | bytes accessed | tf_op | source)
XLA Modules:
  0.0 24.6 jit_solution(10312094152170488071)
XLA Ops:
  0.6 21.8 %shard_map.77 = (f32[4,2,8,256]{3,2,1,0:T(8,128)}, f32[4,8,256]{2,1,0:T(8,128)}) custom-call(bf16[64,256]{1,0:T(8,128)(2,1)} %bitcast.4, bf16[32,256]{1,0:T(8,128)(2,1)} %bitcast.5, bf16[1,4]{1,0:T(2,128)(2,1)} %bitcast.7, f32[8,256]{1,0:T(8,128)} %vel_in.1, f32[8,256]{1,0:T(8,128)} %amp_in.1, s32[2,64]{1,0:T(2,128)} %bitcast.6), custom_call_target="tpu_custom_call" | custom-call | tf_op jit(solution)/shard_map/pallas_call | solution.py:390
  22.5 0.0 copy-start
  22.5 1.5 %copy.10 = f32[4,2,8,256]{3,2,1,0:T(8,128)} copy(f32[4,2,8,256]{3,2,1,0:T(8,128)} %get-tuple-element.4) | data formatting | bytes 131072
  23.9 0.0 copy-done
  23.9 0.6 %copy.11 = f32[4,8,256]{2,1,0:T(8,128)} copy(f32[4,8,256]{2,1,0:T(8,128)S(1)} %copy-done) | data formatting | bytes 65536
Async XLA Ops:
  22.5 1.5 %copy-start = (f32[4,8,256]{2,1,0:T(8,128)S(1)}, f32[4,8,256]{2,1,0:T(8,128)}, u32[]{:S(2)}) copy-start(f32[4,8,256]{2,1,0:T(8,128)} %get-tuple-element.5) | copy-start | bytes 98308

commit v4 on v3

--- a/solution.py
+++ b/solution.py
@@ -156,13 +156,14 @@
         src = vel_ref if which == 0 else amp_ref
         return block_copy(src, vah.at[which], va_send.at[which], va_recv.at[which], core)
 
+    va_copy(0).start()
+    va_copy(1).start()
+    own_copy(1).start()
+    core_copy(me).start()
     for step in range(1, n):
         msg_copy(step).start()
-    for step in range(1, n):
+    for step in range(2, n):
         own_copy(step).start()
-    va_copy(0).start()
-    va_copy(1).start()
-    core_copy(me).start()
 
     at_row = lax.broadcasted_iota(jnp.int32, (2 * cols, cols), 0) % cols
     at_col = lax.broadcasted_iota(jnp.int32, (2 * cols, cols), 1)
@@ -265,11 +266,11 @@
     def chunk(k, carry):
         c = zchunk(k)
 
-        @pl.when(k > 0)
+        @pl.when(k + 1 < zcount)
         def _():
-            forward(k, 0)
-
-        forward(k, 1)
+            forward(k + 1, 0)
+            forward(k + 1, 1)
+
         for s in range(GROUP):
             core_copy(c * GROUP + s).wait_recv()
         unpack(c)
@@ -322,6 +323,7 @@
         lax.fori_loop(0, al, one, 0, unroll=True)
         return carry
 
+    forward(0, 1)
     lax.fori_loop(0, zcount, chunk, 0)
 
     def finish(a, carry):

time: 24.8 us -> 24.2 us (0.976)
  Pallas kernels: 21.8 us -> 21.2 us
    pallas_call x1, Pallas kernels: 21.8 us -> 21.2 us  [per_device(): pl.pallas_call(functools.partial(kernel, n, al, rows, cols, lanes), out_s...]
where the time goes in v4:
time: 24.2 us; the launch traced here: 24 us
  Pallas kernels  21.2 us (88%)
  local copies, waits for them, and re-layouts  2.1 us (9%)
  between operations  0.65 us (3%)
    pallas_call x1, Pallas kernels, per_device(): pl.pallas_call(functools.partial(kernel, n, al, rows, cols, lanes), out_s...  21.2 us
    unnamed x4, local copies, waits for them, and re-layouts  2.1 us

profile of v4, /device:TPU:0, one launch (start us, length us, event | category | flops | bytes accessed | tf_op | source)
XLA Modules:
  0.0 24.0 jit_solution(14480040036425040682)
XLA Ops:
  0.6 21.2 %shard_map.77 = (f32[4,2,8,256]{3,2,1,0:T(8,128)}, f32[4,8,256]{2,1,0:T(8,128)}) custom-call(bf16[64,256]{1,0:T(8,128)(2,1)} %bitcast.4, bf16[32,256]{1,0:T(8,128)(2,1)} %bitcast.5, bf16[1,4]{1,0:T(2,128)(2,1)} %bitcast.7, f32[8,256]{1,0:T(8,128)} %vel_in.1, f32[8,256]{1,0:T(8,128)} %amp_in.1, s32[2,64]{1,0:T(2,128)} %bitcast.6), custom_call_target="tpu_custom_call" | custom-call | tf_op jit(solution)/shard_map/pallas_call | solution.py:392
  21.9 0.0 copy-start
  21.9 1.5 %copy.10 = f32[4,2,8,256]{3,2,1,0:T(8,128)} copy(f32[4,2,8,256]{3,2,1,0:T(8,128)} %get-tuple-element.4) | data formatting | bytes 131072
  23.4 0.0 copy-done
  23.4 0.6 %copy.11 = f32[4,8,256]{2,1,0:T(8,128)} copy(f32[4,8,256]{2,1,0:T(8,128)S(1)} %copy-done) | data formatting | bytes 65536
Async XLA Ops:
  21.9 1.5 %copy-start = (f32[4,8,256]{2,1,0:T(8,128)S(1)}, f32[4,8,256]{2,1,0:T(8,128)}, u32[]{:S(2)}) copy-start(f32[4,8,256]{2,1,0:T(8,128)} %get-tuple-element.5) | copy-start | bytes 98308
